TPU v7x, 32 devices: a whole 2x2x4 slice. The times are simulated.
32 devices in a mesh: section: 2 (over x), row: 4 (over z), col: 4 (over y, core).
Axes of the slice: x: 2, y: 2, z: 4, core: 2. Of those that a mesh axis runs over, the one named last changes fastest.
Arguments:
- streams: bfloat16 [2, 1024, 6144], P('section', 'col', 'row'), may hold values from -6 to 6
- tiles: bfloat16 [2, 6144, 24576], P('section', 'row', 'col'), may hold values from -0.078125 to 0.078125
- order: int32 [8], replicated, may hold values from 0 to 7, each once
Outputs:
- result: bfloat16 [2, 1024, 6144], P('section', 'col', 'row')
Inputs may be any that keep to these rules, and one draw needn't show every extreme that they name: order names every block number once.
All inputs are finite; a program needn't handle non-finite values.
Results may differ from a plain program's by a relative error of at most 0.0054.
Values may be sent and summed in bfloat16 or wider, within the bound.
No kernel may reach another device: no remote copies, remote signals or barrier semaphores. Data moves between devices by JAX's collectives and lax.ppermute only.
A program may use at most 256 MiB of HBM per device.

v0:
```python
import jax
import jax.numpy as jnp
from jax import lax
from jax.sharding import PartitionSpec as P

gelu_scale = 0.7978845608
gelu_cubic = 0.044715


def partner(value, axis, bit):
    mask = 2**bit
    pairs = [(source, source ^ mask) for source in range(lax.axis_size(axis))]
    return lax.ppermute(value, axis, pairs)


def gelu_value(v):
    inner = jnp.tanh(gelu_scale * (v + gelu_cubic * v * v * v))
    return 0.5 * v * (1.0 + inner)


def gelu_slope(v):
    inner = jnp.tanh(gelu_scale * (v + gelu_cubic * v * v * v))
    return 0.5 * (1.0 + inner) + 0.5 * v * (1.0 - inner * inner) * gelu_scale * (
        1.0 + 3.0 * gelu_cubic * v * v
    )


def reorder(rows, index):
    count = index.shape[0]
    shaped = rows.reshape(count, rows.shape[0] // count, rows.shape[1])
    return jnp.take(shaped, index, axis=0).reshape(rows.shape)


def outgoing_of(summed, first_section):
    return jnp.where(first_section, gelu_value(summed), summed).astype(jnp.bfloat16)


def mixed_of(incoming, summed, first_section):
    arrived = incoming.astype(jnp.float32)
    return jnp.where(first_section, arrived * gelu_slope(summed), arrived).astype(jnp.bfloat16)


def per_device(streams, tiles, order):
    first_section = lax.axis_index("section") == 0
    local_rows = streams[0]
    weight_tile = tiles[0]
    count = order.shape[0]
    counter = jnp.arange(count, dtype=jnp.int32)
    inverse = jnp.sum(jnp.where(order[None, :] == counter[:, None], counter[None, :], 0), axis=1)
    first_index = jnp.where(first_section, counter, inverse)
    second_index = jnp.where(first_section, counter, order)
    partial_sums = jnp.dot(
        lax.all_gather(local_rows, "col", axis=0, tiled=True),
        weight_tile,
        preferred_element_type=jnp.float32,
    )
    partial_sums = reorder(partial_sums, first_index)
    summed = lax.psum(partial_sums, "row")
    incoming = partner(outgoing_of(summed, first_section), "section", 0)
    mixed = mixed_of(incoming, summed, first_section)
    product = lax.dot_general(
        mixed, weight_tile, (((1,), (1,)), ((), ())), preferred_element_type=jnp.float32
    )
    product = reorder(product, second_index)
    finished = lax.psum_scatter(product, "col", scatter_dimension=0, tiled=True)
    return finished.astype(jnp.bfloat16)[None]


def solution(mesh):
    placed = (P("section", "col", "row"), P("section", "row", "col"), P())
    return jax.shard_map(
        per_device,
        mesh=mesh,
        in_specs=placed,
        out_specs=P("section", "col", "row"),
        check_vma=False,
    )
```

profile of v0, /device:TPU:0, one launch (start us, length us, event | category | flops | bytes accessed | tf_op | source)
XLA Modules:
  0.0 1350.6 jit_solution(4726055797730773056)
XLA Ops:
  6.5 0.0 all-gather.3.cloned.1.call-start
  6.5 0.7 all-gather.3.cloned.1.call-update
  7.3 0.0 all-reduce.2.cloned.1.call-start
  7.3 0.8 select_reduce_fusion
  8.1 0.1 broadcast_bitcast_fusion
  8.2 32.0 %all-gather.3.cloned.1.call-done = bf16[1,1024,1536]{2,1,0:T(8,128)(2,1)} async-done(((bf16[1,256,1536]{2,1,0:T(8,128)(2,1)}), bf16[1,1024,1536]{2,1,0:T(8,128)(2,1)}) %all-gather.3.cloned.1.call-update) | async-done | bytes 3145744 | tf_op jit(solution)/shard_map/all_gather | solution.py:53
  40.2 26.2 %fusion.8 = f32[8,128,6144]{2,1,0:T(8,128)} fusion(bf16[8,128,1536]{2,1,0:T(8,128)(2,1)} %bitcast.27, bf16[1,1536,6144]{2,1,0:T(8,128)(2,1)} %param.4), kind=kOutput, calls=%fused_computation.15 | convolution fusion | flops 19327352832 | bytes 47185920 | tf_op jit(solution)/shard_map/dot_general | solution.py:52
  66.4 18.4 %gather_fusion = f32[8,128,6144]{2,1,0:T(8,128)} fusion(f32[8,128,6144]{2,1,0:T(8,128)} %fusion.8, s32[1024]{0:T(1024)S(1)} %pad_clamp_fusion.1), kind=kCustom, calls=%fused_computation | custom fusion | bytes 50331680 | tf_op jit(solution)/shard_map/jit(_take)/gather | solution.py:31
  84.8 17.5 %bitcast_select_fusion = f32[1024,6144]{1,0:T(8,128)} fusion(f32[8,128,6144]{2,1,0:T(8,128)} %gather_fusion, pred[1024]{0:T(1024)(128)(4,1)S(1)} %broadcast_bitcast_fusion), kind=kLoop, calls=%fused_computation.11 | loop fusion | flops 6291456 | bytes 50332672 | tf_op jit(solution)/shard_map/jit(_take)/select_n | solution.py:31
  102.3 0.0 all-reduce.2.cloned.1.call-update
  102.3 0.0 copy-start.1
  102.4 0.2 reduce-scatter.2.cloned.1.call-start
  102.6 832.6 %all-reduce.2.cloned.1.call-done = f32[1024,6144]{1,0:T(8,128)} async-done(((f32[1024,6144]{1,0:T(8,128)}), f32[1024,6144]{1,0:T(8,128)}) %all-reduce.2.cloned.1.call-update) | async-done | bytes 25165840 | tf_op jit(solution)/shard_map/psum | solution.py:58
  935.2 17.7 %select_convert_fusion = bf16[1024,6144]{1,0:T(8,128)(2,1)} fusion(f32[1024,6144]{1,0:T(8,128)} %all-reduce.2.cloned.1.call-done, pred[]{:T(512)S(6)} %eq.16), kind=kLoop, calls=%fused_computation.12 | loop fusion | flops 62914560 | bytes 37748736 | tf_op jit(solution)/shard_map/convert_element_type | solution.py:35
  952.9 1.5 collective-permute-start
  954.4 0.1 broadcast_bitcast_fusion.1
  954.5 270.8 %collective-permute-done = bf16[1024,6144]{1,0:T(8,128)(2,1)} collective-permute-done((bf16[1024,6144]{1,0:T(8,128)(2,1)}, bf16[1024,6144]{1,0:T(8,128)(2,1)}, u32[]{:S(2)}, u32[]{:S(2)}) %collective-permute-start) | collective-permute-done | bytes 12582944 | tf_op jit(solution)/shard_map/ppermute | solution.py:13
  1225.3 20.2 %fusion.5 = bf16[1024,6144]{1,0:T(8,128)(2,1)} fusion(f32[1024,6144]{1,0:T(8,128)S(1)} %copy-done, bf16[1024,6144]{1,0:T(8,128)(2,1)} %collective-permute-done, pred[]{:T(512)S(6)} %eq.16), kind=kLoop, calls=%fused_computation.10 | loop fusion | flops 132120576 | bytes 50331648 | tf_op jit(solution)/shard_map/convert_element_type | solution.py:40
  1245.5 26.3 %fusion.6 = f32[8,128,1536]{2,1,0:T(8,128)} fusion(bf16[8,128,6144]{2,1,0:T(8,128)(2,1)} %bitcast.26, bf16[1,1536,6144]{2,1,0:T(8,128)(2,1)} %param.4), kind=kOutput, calls=%fused_computation.13 | convolution fusion | flops 19327352832 | bytes 37748736 | tf_op jit(solution)/shard_map/dot_general | solution.py:61
  1271.8 6.4 gather_fusion.1
  1278.2 5.9 bitcast_select_fusion.1
  1284.1 0.0 reduce-scatter.2.cloned.1.call-update
  1284.1 57.5 %reduce-scatter.2.cloned.1.call-done = f32[256,1536]{1,0:T(8,128)} async-done(((f32[1024,1536]{1,0:T(8,128)}), f32[256,1536]{1,0:T(8,128)}) %reduce-scatter.2.cloned.1.call-update) | async-done | bytes 1572880 | tf_op jit(solution)/shard_map/reduce_scatter | solution.py:65
  1341.7 2.4 convert_bitcast_fusion
  (8 shorter events, 0.0 us)
Async XLA Ops:
  6.5 33.6 %all-gather.3.cloned.1.call-start = ((), (), s32[]{:S(2)}) async-start(), calls=%async_computation.3 | async-start | bytes 3932160 | tf_op jit(solution)/shard_map/all_gather | solution.py:53
  7.3 927.9 %all-reduce.2.cloned.1.call-start = ((), (), s32[]{:S(2)}) async-start(), calls=%async_computation.1 | async-start | bytes 50331648 | tf_op jit(solution)/shard_map/psum | solution.py:58
  102.3 852.0 %copy-start.1 = (s32[8]{0:T(128)S(1)}, s32[8]{0:T(128)}, u32[]{:S(2)}) copy-start(s32[8]{0:T(128)} %param.5) | copy-start | bytes 100
  102.4 1239.3 %reduce-scatter.2.cloned.1.call-start = ((), (), s32[]{:S(2)}) async-start(), calls=%async_computation.2 | async-start | bytes 7864320 | tf_op jit(solution)/shard_map/reduce_scatter | solution.py:65
  935.2 290.1 %copy-start = (f32[1024,6144]{1,0:T(8,128)S(1)}, f32[1024,6144]{1,0:T(8,128)}, u32[]{:S(2)}) copy-start(f32[1024,6144]{1,0:T(8,128)} %all-reduce.2.cloned.1.call-done) | copy-start | bytes 75497472
  952.9 272.4 %collective-permute-start = (bf16[1024,6144]{1,0:T(8,128)(2,1)}, bf16[1024,6144]{1,0:T(8,128)(2,1)}, u32[]{:S(2)}, u32[]{:S(2)}) collective-permute-start(bf16[1024,6144]{1,0:T(8,128)(2,1)} %select_convert_fusion), channel_id=1, source_target_pairs={{0,16},{16,0},{1,17},{17,1},{2,18},{18,2},{3,19},{19,3},{4,20},{20... | collective-permute-start | bytes 37748744 | tf_op jit(solution)/shard_map/ppermute | solution.py:13
Sparse Core Ops, SparseCore 0:
  8.9 31.2 all-gather.2
  102.5 832.6 all-reduce.1
  1284.3 57.3 reduce-scatter.1
where the time goes:
time: 1350 us
  waiting for transfers between devices  1190 us (88%)
  other arithmetic  64.5 us (5%)
  matrix products  52.5 us (4%)
  local copies, waits for them, and re-layouts  25 us (2%)
    psum x1, waiting for transfers between devices, per_device(): summed = lax.psum(partial_sums, 'row')  833 us
    ppermute x1, waiting for transfers between devices, partner(): return lax.ppermute(value, axis, pairs)  271 us
    reduce_scatter x1, waiting for transfers between devices, per_device(): finished = lax.psum_scatter(product, 'col', scatter_dimension=0, tiled=True)  57.5 us
    all_gather x1, waiting for transfers between devices, per_device(): lax.all_gather(local_rows, 'col', axis=0, tiled=True)  32 us
  transfers between devices with their start and end apart: 4, of which 4 were waited for; matrix products, arithmetic and copies ran while one was open for 0% of the time, Pallas kernels for 0%

commit v1 on v0

v1 whole, which is shorter than its diff:
```python
import jax
import jax.numpy as jnp
from jax import lax
from jax.sharding import PartitionSpec as P

gelu_scale = 0.7978845608
gelu_cubic = 0.044715
COLUMN_CHUNKS = 4
TOKEN_GROUPS = 4
SKEW = 2


def partner(value, axis, bit):
    mask = 2**bit
    pairs = [(source, source ^ mask) for source in range(lax.axis_size(axis))]
    return lax.ppermute(value, axis, pairs)


def gelu_value(v):
    inner = jnp.tanh(gelu_scale * (v + gelu_cubic * v * v * v))
    return 0.5 * v * (1.0 + inner)


def gelu_slope(v):
    inner = jnp.tanh(gelu_scale * (v + gelu_cubic * v * v * v))
    return 0.5 * (1.0 + inner) + 0.5 * v * (1.0 - inner * inner) * gelu_scale * (
        1.0 + 3.0 * gelu_cubic * v * v
    )


def gather_rows(own, bits):
    shards, masks = [own], [0]
    for bit in reversed(range(bits)):
        shards = shards + [partner(shard, "col", bit) for shard in shards]
        masks = masks + [mask ^ (1 << bit) for mask in masks]
    return shards, masks


def scatter_sum(partials, col, bits):
    held = partials
    for bit in range(bits):
        pairs = held.reshape(held.shape[0] // 2, 2, *held.shape[1:])
        mine = (col >> bit) & 1
        keep = jnp.where(mine == 0, pairs[:, 0], pairs[:, 1])
        give = jnp.where(mine == 0, pairs[:, 1], pairs[:, 0])
        if bit > 0:
            give = give.astype(jnp.bfloat16)
        held = keep + partner(give, "col", bit).astype(jnp.float32)
    return held[0]


def per_device(streams, tiles, order):
    row_size, col_size = lax.axis_size("row"), lax.axis_size("col")
    row, col = lax.axis_index("row"), lax.axis_index("col")
    first_section = lax.axis_index("section") == 0
    bits = col_size.bit_length() - 1
    own_rows, weight = streams[0], tiles[0]
    local, depth = own_rows.shape
    tokens = local * col_size
    half = weight.shape[1] // 2
    chunks, groups = COLUMN_CHUNKS, TOKEN_GROUPS
    chunk = half // chunks
    group_rows = tokens // groups
    unit = local // groups
    block = tokens // order.shape[0]
    last = row_size - 1

    shards, masks = gather_rows(own_rows, bits)
    place = [masks.index(g) for g in range(col_size)]
    place = jnp.array(place, jnp.int32)
    per_block = block // unit
    counter = jnp.arange(order.shape[0], dtype=jnp.int32)
    inverse = jnp.sum(jnp.where(order[None, :] == counter[:, None], counter[None, :], 0), axis=1)
    moved = jnp.where(first_section, inverse, order)
    units = jnp.arange(tokens // unit, dtype=jnp.int32)
    source = jnp.take(moved, units // per_block) * per_block + units % per_block

    def position(index):
        return jnp.take(place, (index // groups) ^ col) * groups + index % groups

    own_place, other_place = position(units), position(source)

    each = col_size // groups
    if each > 1:
        grouped = [jnp.concatenate(shards[i * each : (i + 1) * each]) for i in range(groups)]
    else:
        grouped = shards
    stacked = jnp.stack(grouped)

    pieces = [(0, j) for j in range(chunks)]
    pieces += [(g, j) for j in range(chunks) for g in range(1, groups)]
    count = len(pieces)
    group_of = jnp.array([g for g, _ in pieces], jnp.int32)
    chunk_of = jnp.array([j for _, j in pieces], jnp.int32)
    sends = [(t, j) for j in range(chunks // 2) for t in range(groups)]
    sends += [(t, j) for t in range(groups) for j in range(chunks // 2, chunks)]
    right = [(d, d + 1) for d in range(last)]
    left = [(d + 1, d) for d in range(last)]

    def partial_sum(slot, start, offset):
        index = jnp.clip(slot - start, 0, count - 1)
        if slot < chunks:
            rows = grouped[0]
        else:
            rows = lax.dynamic_index_in_dim(stacked, group_of[index], 0, keepdims=False)
        columns = lax.dynamic_slice_in_dim(weight, offset + chunk_of[index] * chunk, chunk, 1)
        sums = jnp.dot(rows, columns, preferred_element_type=jnp.float32)
        if slot >= count:
            sums = jnp.where(slot - start < count, sums, 0.0)
        return sums

    starts = (SKEW * row, SKEW * (last - row))
    ends = (row == 0, row == last)
    offsets = (0, half)
    paths = (right, left)
    arrived = ({}, {})
    held = ({}, {})
    pre, incoming, mixed = {}, {}, {}
    depth_slots = SKEW * last
    ready = [max(i for i, (_, k) in enumerate(pieces) if k == j) for j in range(chunks)]
    back = max(depth_slots + ready[j] + 2 - i for i, (_, j) in enumerate(sends))
    back = max(back, count)
    slots = back + count + depth_slots
    product = [None] * groups
    finished = [None] * groups

    def mix(j):
        theirs = jnp.concatenate([incoming[pieces.index((g, j))] for g in range(groups)])
        theirs = theirs.reshape(-1, unit, chunk)
        ours = jnp.concatenate([pre[pieces.index((g, j))] for g in range(groups)])
        ours = ours.reshape(-1, unit, chunk)
        for t in range(groups):
            a = jnp.take(theirs, other_place[t::groups], axis=0).astype(jnp.float32)
            v = jnp.take(ours, own_place[t::groups], axis=0)
            m = jnp.where(first_section, a * gelu_slope(v), a).astype(jnp.bfloat16)
            mixed[(t, j)] = m.reshape(group_rows, chunk)

    for slot in range(slots):
        totals = [None, None]
        for way in range(2):
            base = arrived[way].get(slot - SKEW)
            if back <= slot < back + count:
                base = jnp.where(ends[way], mixed[sends[slot - back]], base)
            if slot < count + depth_slots:
                sums = partial_sum(slot, starts[way], offsets[way])
                if base is not None:
                    sums = base.astype(jnp.float32) + sums
                totals[way] = sums
                base = sums.astype(jnp.bfloat16)
            held[way][slot] = base
            if slot < slots - SKEW:
                arrived[way][slot] = lax.ppermute(base, "row", paths[way])
        index = slot - depth_slots
        if 0 <= index < count:
            total = jnp.where(row == 0, totals[1], totals[0])
            pre[index] = total
            outgoing = jnp.where(first_section, gelu_value(total), total).astype(jnp.bfloat16)
            incoming[index] = partner(outgoing, "section", 0)
            for j in range(chunks):
                if index == ready[j]:
                    mix(j)
        index = slot - depth_slots - back
        if index >= 0:
            t, j = sends[index]
            for way in range(2):
                value = held[way][back + index + SKEW * last]
                for d in range(last):
                    ahead = SKEW * (d if way == 0 else d)
                    here = row == (d if way == 0 else last - d)
                    value = jnp.where(here, held[way][back + index + ahead], value)
                begin = offsets[1 - way] + j * chunk
                term = lax.dot_general(
                    value,
                    weight[:, begin : begin + chunk],
                    (((1,), (1,)), ((), ())),
                    preferred_element_type=jnp.float32,
                )
                product[t] = term if product[t] is None else product[t] + term
            if index == max(i for i, (u, _) in enumerate(sends) if u == t):
                parts = product[t].reshape(col_size, unit, depth)
                finished[t] = scatter_sum(parts, col, bits).astype(jnp.bfloat16)
    return jnp.concatenate(finished)[None]


def solution(mesh):
    placed = (P("section", "col", "row"), P("section", "row", "col"), P())
    return jax.shard_map(
        per_device,
        mesh=mesh,
        in_specs=placed,
        out_specs=P("section", "col", "row"),
        check_vma=False,
    )
```

time: 1350 us -> 760 us (0.56); the launches traced: 1350 us -> 746 us
  waiting for transfers between devices: 1190 us -> 38.3 us
  starting transfers between devices: 1.73 us -> 242 us
  matrix products: 52.5 us -> 185 us
  local copies, waits for them, and re-layouts: 25 us -> 115 us
  between operations: 13.1 us -> 99.5 us
    psum x1 -> x0, waiting for transfers between devices: 833 us -> none  [per_device(): summed = lax.psum(partial_sums, 'row')]
    ppermute x1 -> x27, waiting for transfers between devices: 271 us -> 10.2 us  [partner(): return lax.ppermute(value, axis, pairs)]
    ppermute x0 -> x72, starting transfers between devices: none -> 220 us  [per_device(): arrived[way][slot] = lax.ppermute(base, 'row', paths[way])]
    dot_general x2 -> x76, matrix products: 52.5 us -> 185 us  [the longest x44 116 us: partial_sum(): sums = jnp.dot(rows, columns, preferred_element_type=jnp.float32)]
    reduce_scatter x1 -> x0, waiting for transfers between devices: 57.5 us -> none  [per_device(): finished = lax.psum_scatter(product, 'col', scatter_dimension=0, tiled=True)]
    gather x2 -> x35, local copies, waits for them, and re-layouts: 24.8 us -> 70 us  [the longest x16 34.1 us: mix(): a = jnp.take(theirs, other_place[t::groups], axis=0).astype(jnp.float32)]
    all_gather x1 -> x0, waiting for transfers between devices: 32 us -> none  [per_device(): lax.all_gather(local_rows, 'col', axis=0, tiled=True)]
    ppermute x0 -> x72, waiting for transfers between devices: none -> 28.1 us  [per_device(): arrived[way][slot] = lax.ppermute(base, 'row', paths[way])]
  transfers between devices with their start and end apart: 4 -> 99, of which waited for: 4 -> 15; matrix products, arithmetic and copies ran while one was open for 0% -> 49% of each run, Pallas kernels for 0% -> 0%
where the time goes in v1:
time: 760 us; the launch traced here: 746 us
  starting transfers between devices  242 us (32%)
  matrix products  185 us (24%)
  local copies, waits for them, and re-layouts  115 us (15%)
  between operations  99.5 us (13%)
  other arithmetic  66.5 us (9%)
  waiting for transfers between devices  38.3 us (5%)
    ppermute x72, starting transfers between devices, per_device(): arrived[way][slot] = lax.ppermute(base, 'row', paths[way])  220 us
    dot_general x44, matrix products, partial_sum(): sums = jnp.dot(rows, columns, preferred_element_type=jnp.float32)  116 us
    dot_general x32, matrix products, per_device(): lax.dot_general(value, weight[:, begin:begin + chunk], (((1,), (1,)), (()...  69.1 us
    gather x16, local copies, waits for them, and re-layouts, mix(): a = jnp.take(theirs, other_place[t::groups], axis=0).astype(jnp.float32)  34.1 us
    gather x16, local copies, waits for them, and re-layouts, mix(): v = jnp.take(ours, own_place[t::groups], axis=0)  34 us
    ppermute x72, waiting for transfers between devices, per_device(): arrived[way][slot] = lax.ppermute(base, 'row', paths[way])  28.1 us
    convert_element_type x9, other arithmetic, mix(): m = jnp.where(first_section, a * gelu_slope(v), a).astype(jnp.bfloat16)  25.1 us
    ppermute x27, starting transfers between devices, partner(): return lax.ppermute(value, axis, pairs)  22.1 us
  transfers between devices with their start and end apart: 99, of which 15 were waited for; matrix products, arithmetic and copies ran while one was open for 49% of the time, Pallas kernels for 0%

profile of v1, /device:TPU:0, one launch (start us, length us, event | category | flops | bytes accessed | tf_op | source)
XLA Modules:
  0.0 746.0 jit_solution(8719188580605869445)
XLA Ops:
  23.3 5.3 collective-permute-start.6
  140.1 4.8 collective-permute-start.25
  151.4 4.8 collective-permute-start.7
  165.7 4.7 collective-permute-start.26
  178.3 8.5 %collective-permute-done.8 = bf16[256,768]{0,1:T(8,128)(2,1)S(1)} collective-permute-done((bf16[256,768]{0,1:T(8,128)(2,1)S(1)}, bf16[256,768]{0,1:T(8,128)(2,1)S(1)}, u32[]{:S(2)}, u32[]{:S(2)}) %collective-permute-start.8) | collective-permute-done | bytes 393248 | tf_op jit(solution)/shard_map/ppermute | solution.py:152
  249.1 5.3 collective-permute-start.33
  279.0 5.3 collective-permute-start.30
  315.4 5.3 collective-permute-start.39
  322.1 5.3 collective-permute-start.50
  405.0 5.4 collective-permute-start.63
  411.7 5.3 collective-permute-start.41
  442.9 5.5 collective-permute-start.67
  471.0 5.4 collective-permute-start.69
  507.2 5.3 collective-permute-start.42
  553.4 6.9 collective-permute-start.70
  594.1 4.7 collective-permute-start.72
  615.3 4.7 collective-permute-start.73
  636.0 5.6 collective-permute-start.83
  649.1 5.3 collective-permute-start.81
  678.1 4.8 collective-permute-start.89
  684.3 4.8 collective-permute-start.87
  693.7 5.5 collective-permute-done.88
  709.4 5.3 collective-permute-start.95
  735.8 4.9 collective-permute-done.92
  (599 shorter events, 517.6 us)
Async XLA Ops:
  0.0 144.9 %collective-permute-start.2 = (bf16[256,1536]{1,0:T(8,128)(2,1)}, bf16[256,1536]{1,0:T(8,128)(2,1)}, u32[]{:S(2)}, u32[]{:S(2)}) collective-permute-start(bf16[256,1536]{1,0:T(8,128)(2,1)} %bitcast.831), channel_id=1, source_target_pairs={{0,2},{1,3},{2,0},{3,1},{4,6},{5,7},{6,4},{7,5},{8,10},{9,11},{10,... | collective-permute-start | bytes 2359304 | tf_op jit(solution)/shard_map/ppermute | solution.py:16
  3.0 155.8 %collective-permute-start.3 = (bf16[256,1536]{1,0:T(8,128)(2,1)}, bf16[256,1536]{1,0:T(8,128)(2,1)}, u32[]{:S(2)}, u32[]{:S(2)}) collective-permute-start(bf16[256,1536]{1,0:T(8,128)(2,1)} %bitcast.832), channel_id=1, source_target_pairs={{0,1},{1,0},{2,3},{3,2},{4,5},{5,4},{6,7},{7,6},{8,9},{9,8},{10,11... | collective-permute-start | bytes 2359304 | tf_op jit(solution)/shard_map/ppermute | solution.py:16
  9.2 126.8 %collective-permute-start.24 = (bf16[256,768]{0,1:T(8,128)(2,1)}, bf16[256,768]{0,1:T(8,128)(2,1)}, u32[]{:S(2)}, u32[]{:S(2)}) collective-permute-start(bf16[256,768]{0,1:T(8,128)(2,1)} %fusion.390), channel_id=1, source_target_pairs={{0,4},{4,8},{8,12},{1,5},{5,9},{9,13},{2,6},{6,10},{10,14},{3,7},{... | collective-permute-start | bytes 1179656 | tf_op jit(solution)/shard_map/ppermute | solution.py:152
  17.3 122.8 %collective-permute-start.17 = (bf16[256,768]{0,1:T(8,128)(2,1)}, bf16[256,768]{0,1:T(8,128)(2,1)S(1)}, u32[]{:S(2)}, u32[]{:S(2)}) collective-permute-start(bf16[256,768]{0,1:T(8,128)(2,1)} %fusion.393), channel_id=1, source_target_pairs={{4,0},{8,4},{12,8},{5,1},{9,5},{13,9},{6,2},{10,6},{14,10},{7,3},{... | collective-permute-start | bytes 1179656 | tf_op jit(solution)/shard_map/ppermute | solution.py:152
  23.3 124.2 %collective-permute-start.6 = (bf16[256,768]{0,1:T(8,128)(2,1)}, bf16[256,768]{0,1:T(8,128)(2,1)}, u32[]{:S(2)}, u32[]{:S(2)}) collective-permute-start(bf16[256,768]{0,1:T(8,128)(2,1)} %fusion.396), channel_id=1, source_target_pairs={{0,4},{4,8},{8,12},{1,5},{5,9},{9,13},{2,6},{6,10},{10,14},{3,7},{... | collective-permute-start | bytes 1179656 | tf_op jit(solution)/shard_map/ppermute | solution.py:152
  204.9 73.5 %collective-permute-start.35 = (bf16[256,768]{0,1:T(8,128)(2,1)}, bf16[256,768]{0,1:T(8,128)(2,1)S(1)}, u32[]{:S(2)}, u32[]{:S(2)}) collective-permute-start(bf16[256,768]{0,1:T(8,128)(2,1)} %get-tuple-element.24), channel_id=1, source_target_pairs={{0,16},{16,0},{1,17},{17,1},{2,18},{18,2},{3,19},{19,3},{4,20},{20... | collective-permute-start | bytes 1179656 | tf_op jit(solution)/shard_map/ppermute | solution.py:16
  243.2 35.8 %collective-permute-start.37 = (bf16[256,768]{0,1:T(8,128)(2,1)}, bf16[256,768]{0,1:T(8,128)(2,1)}, u32[]{:S(2)}, u32[]{:S(2)}) collective-permute-start(bf16[256,768]{0,1:T(8,128)(2,1)} %get-tuple-element.28), channel_id=1, source_target_pairs={{0,16},{16,0},{1,17},{17,1},{2,18},{18,2},{3,19},{19,3},{4,20},{20... | collective-permute-start | bytes 1179656 | tf_op jit(solution)/shard_map/ppermute | solution.py:16
  244.9 39.4 %collective-permute-start.36 = (bf16[256,768]{0,1:T(8,128)(2,1)}, bf16[256,768]{0,1:T(8,128)(2,1)}, u32[]{:S(2)}, u32[]{:S(2)}) collective-permute-start(bf16[256,768]{0,1:T(8,128)(2,1)} %get-tuple-element.26), channel_id=1, source_target_pairs={{0,16},{16,0},{1,17},{17,1},{2,18},{18,2},{3,19},{19,3},{4,20},{20... | collective-permute-start | bytes 1179656 | tf_op jit(solution)/shard_map/ppermute | solution.py:16
  272.4 43.0 %collective-permute-start.9 = (bf16[256,768]{0,1:T(8,128)(2,1)}, bf16[256,768]{0,1:T(8,128)(2,1)}, u32[]{:S(2)}, u32[]{:S(2)}) collective-permute-start(bf16[256,768]{0,1:T(8,128)(2,1)} %get-tuple-element.34), channel_id=1, source_target_pairs={{0,16},{16,0},{1,17},{17,1},{2,18},{18,2},{3,19},{19,3},{4,20},{20... | collective-permute-start | bytes 1179656 | tf_op jit(solution)/shard_map/ppermute | solution.py:16
  278.5 126.5 %collective-permute-start.47 = (bf16[256,768]{0,1:T(8,128)(2,1)}, bf16[256,768]{0,1:T(8,128)(2,1)}, u32[]{:S(2)}, u32[]{:S(2)}) collective-permute-start(bf16[256,768]{0,1:T(8,128)(2,1)} %get-tuple-element.6), channel_id=1, source_target_pairs={{0,16},{16,0},{1,17},{17,1},{2,18},{18,2},{3,19},{19,3},{4,20},{20... | collective-permute-start | bytes 1179656 | tf_op jit(solution)/shard_map/ppermute | solution.py:16
  363.1 47.3 %collective-permute-start.51 = (bf16[256,768]{0,1:T(8,128)(2,1)}, bf16[256,768]{0,1:T(8,128)(2,1)}, u32[]{:S(2)}, u32[]{:S(2)}) collective-permute-start(bf16[256,768]{0,1:T(8,128)(2,1)} %get-tuple-element.12), channel_id=1, source_target_pairs={{0,16},{16,0},{1,17},{17,1},{2,18},{18,2},{3,19},{19,3},{4,20},{20... | collective-permute-start | bytes 1179656 | tf_op jit(solution)/shard_map/ppermute | solution.py:16
  363.6 48.0 %collective-permute-start.48 = (bf16[256,768]{0,1:T(8,128)(2,1)}, bf16[256,768]{0,1:T(8,128)(2,1)}, u32[]{:S(2)}, u32[]{:S(2)}) collective-permute-start(bf16[256,768]{0,1:T(8,128)(2,1)} %get-tuple-element.10), channel_id=1, source_target_pairs={{0,16},{16,0},{1,17},{17,1},{2,18},{18,2},{3,19},{19,3},{4,20},{20... | collective-permute-start | bytes 1179656 | tf_op jit(solution)/shard_map/ppermute | solution.py:16
  372.2 44.8 %collective-permute-start.52 = (bf16[256,768]{0,1:T(8,128)(2,1)}, bf16[256,768]{0,1:T(8,128)(2,1)}, u32[]{:S(2)}, u32[]{:S(2)}) collective-permute-start(bf16[256,768]{0,1:T(8,128)(2,1)} %get-tuple-element.14), channel_id=1, source_target_pairs={{0,16},{16,0},{1,17},{17,1},{2,18},{18,2},{3,19},{19,3},{4,20},{20... | collective-permute-start | bytes 1179656 | tf_op jit(solution)/shard_map/ppermute | solution.py:16
  373.3 103.0 %collective-permute-start.61 = (bf16[256,768]{0,1:T(8,128)(2,1)}, bf16[256,768]{0,1:T(8,128)(2,1)}, u32[]{:S(2)}, u32[]{:S(2)}) collective-permute-start(bf16[256,768]{0,1:T(8,128)(2,1)} %get-tuple-element.16), channel_id=1, source_target_pairs={{0,16},{16,0},{1,17},{17,1},{2,18},{18,2},{3,19},{19,3},{4,20},{20... | collective-permute-start | bytes 1179656 | tf_op jit(solution)/shard_map/ppermute | solution.py:16
  411.7 40.2 %collective-permute-start.41 = (bf16[256,768]{0,1:T(8,128)(2,1)}, bf16[256,768]{0,1:T(8,128)(2,1)}, u32[]{:S(2)}, u32[]{:S(2)}) collective-permute-start(bf16[256,768]{0,1:T(8,128)(2,1)} %get-tuple-element.50), channel_id=1, source_target_pairs={{0,4},{4,8},{8,12},{1,5},{5,9},{9,13},{2,6},{6,10},{10,14},{3,7},{... | collective-permute-start | bytes 1179656 | tf_op jit(solution)/shard_map/ppermute | solution.py:152
  417.0 37.6 %collective-permute-start.45 = (bf16[256,768]{0,1:T(8,128)(2,1)}, bf16[256,768]{0,1:T(8,128)(2,1)}, u32[]{:S(2)}, u32[]{:S(2)}) collective-permute-start(bf16[256,768]{0,1:T(8,128)(2,1)} %get-tuple-element.51), channel_id=1, source_target_pairs={{4,0},{8,4},{12,8},{5,1},{9,5},{13,9},{6,2},{10,6},{14,10},{7,3},{... | collective-permute-start | bytes 1179656 | tf_op jit(solution)/shard_map/ppermute | solution.py:152
  461.0 46.2 %collective-permute-start.65 = (bf16[256,768]{0,1:T(8,128)(2,1)}, bf16[256,768]{0,1:T(8,128)(2,1)}, u32[]{:S(2)}, u32[]{:S(2)}) collective-permute-start(bf16[256,768]{0,1:T(8,128)(2,1)} %get-tuple-element.20), channel_id=1, source_target_pairs={{0,16},{16,0},{1,17},{17,1},{2,18},{18,2},{3,19},{19,3},{4,20},{20... | collective-permute-start | bytes 1179656 | tf_op jit(solution)/shard_map/ppermute | solution.py:16
  461.5 51.0 %collective-permute-start.64 = (bf16[256,768]{0,1:T(8,128)(2,1)}, bf16[256,768]{0,1:T(8,128)(2,1)}, u32[]{:S(2)}, u32[]{:S(2)}) collective-permute-start(bf16[256,768]{0,1:T(8,128)(2,1)} %get-tuple-element.18), channel_id=1, source_target_pairs={{0,16},{16,0},{1,17},{17,1},{2,18},{18,2},{3,19},{19,3},{4,20},{20... | collective-permute-start | bytes 1179656 | tf_op jit(solution)/shard_map/ppermute | solution.py:16
  470.5 43.3 %collective-permute-start.68 = (bf16[256,768]{0,1:T(8,128)(2,1)}, bf16[256,768]{0,1:T(8,128)(2,1)}, u32[]{:S(2)}, u32[]{:S(2)}) collective-permute-start(bf16[256,768]{0,1:T(8,128)(2,1)} %get-tuple-element.22), channel_id=1, source_target_pairs={{0,16},{16,0},{1,17},{17,1},{2,18},{18,2},{3,19},{19,3},{4,20},{20... | collective-permute-start | bytes 1179656 | tf_op jit(solution)/shard_map/ppermute | solution.py:16
  471.0 51.1 %collective-permute-start.69 = (bf16[256,768]{0,1:T(8,128)(2,1)S(1)}, bf16[256,768]{0,1:T(8,128)(2,1)}, u32[]{:S(2)}, u32[]{:S(2)}) collective-permute-start(bf16[256,768]{0,1:T(8,128)(2,1)S(1)} %get-tuple-element.52), channel_id=1, source_target_pairs={{0,4},{4,8},{8,12},{1,5},{5,9},{9,13},{2,6},{6,10},{10,14},{3,7},{... | collective-permute-start | bytes 1179656 | tf_op jit(solution)/shard_map/ppermute | solution.py:152
  476.4 45.8 %collective-permute-start.74 = (bf16[256,768]{0,1:T(8,128)(2,1)}, bf16[256,768]{0,1:T(8,128)(2,1)}, u32[]{:S(2)}, u32[]{:S(2)}) collective-permute-start(bf16[256,768]{0,1:T(8,128)(2,1)} %get-tuple-element.53), channel_id=1, source_target_pairs={{4,0},{8,4},{12,8},{5,1},{9,5},{13,9},{6,2},{10,6},{14,10},{7,3},{... | collective-permute-start | bytes 1179656 | tf_op jit(solution)/shard_map/ppermute | solution.py:152
  524.0 50.0 %collective-permute-start.75 = (bf16[256,768]{0,1:T(8,128)(2,1)}, bf16[256,768]{0,1:T(8,128)(2,1)}, u32[]{:S(2)}, u32[]{:S(2)}) collective-permute-start(bf16[256,768]{0,1:T(8,128)(2,1)} %get-tuple-element.93), channel_id=1, source_target_pairs={{4,0},{8,4},{12,8},{5,1},{9,5},{13,9},{6,2},{10,6},{14,10},{7,3},{... | collective-permute-start | bytes 1179656 | tf_op jit(solution)/shard_map/ppermute | solution.py:152
  532.0 51.9 %collective-permute-start.55 = (bf16[256,768]{0,1:T(8,128)(2,1)}, bf16[256,768]{0,1:T(8,128)(2,1)}, u32[]{:S(2)}, u32[]{:S(2)}) collective-permute-start(bf16[256,768]{0,1:T(8,128)(2,1)} %get-tuple-element.83), channel_id=1, source_target_pairs={{4,0},{8,4},{12,8},{5,1},{9,5},{13,9},{6,2},{10,6},{14,10},{7,3},{... | collective-permute-start | bytes 1179656 | tf_op jit(solution)/shard_map/ppermute | solution.py:152
  676.6 39.5 %collective-permute-start.85 = (f32[2,64,1536]{2,1,0:T(8,128)}, f32[2,64,1536]{2,1,0:T(8,128)}, u32[]{:S(2)}, u32[]{:S(2)}) collective-permute-start(f32[2,64,1536]{2,1,0:T(8,128)} %select_bitcast_fusion.2), channel_id=1, source_target_pairs={{0,1},{1,0},{2,3},{3,2},{4,5},{5,4},{6,7},{7,6},{8,9},{9,8},{10,11... | collective-permute-start | bytes 2359304 | tf_op jit(solution)/shard_map/ppermute | solution.py:16
  (176 other events, 2610.8 us)
